TPU v7x, 32 devices: a whole 2x2x4 slice. The times are simulated.
32 devices in a mesh: clip: 4 (over y, core), tm: 2 (over x), height: 4 (over z).
Axes of the slice: x: 2, y: 2, z: 4, core: 2. Of those that a mesh axis runs over, the one named last changes fastest.
Arguments:
- pixels: bfloat16 [16, 3, 4, 4, 384], P('clip', None, 'tm', 'height'), may hold values from -6 to 6
- lengths: int32 [16], replicated, may hold values from 2 to 4, as said below
- route: int32 [16], replicated, may hold values from 0 to 3, as said below
- w_in: bfloat16 [96, 3, 3, 3, 3], replicated, may hold values from -0.625 to 0.625
- b_in: float32 [96], replicated, may hold values from -3 to 3
- gain: float32 [96], replicated, may hold values from 0.1 to 1.9
- w_mid: bfloat16 [96, 96, 3, 3, 3], replicated, may hold values from -0.125 to 0.125
- b_mid: float32 [96], replicated, may hold values from -3 to 3
Outputs:
- features: bfloat16 [16, 96, 4, 4, 384], P('clip', None, 'tm', 'height')
Inputs may be any that keep to these rules, and one draw needn't show every extreme that they name: `lengths`: some clip has 4 frames and some clip has 2. `route`: in each aligned block of 4 clips every value 0 to 3 appears exactly once; the lists are chosen from the lengths so that the frame totals of the clip devices are close.
All inputs are finite; a program needn't handle non-finite values.
Results may differ from a plain program's by a relative error of at most 0.009.
Values may be sent and summed in bfloat16 or wider, within the bound.
A program may use at most 64 MiB of HBM per device.

v0:
```python
import jax
import jax.numpy as jnp
from jax import lax
from jax.sharding import PartitionSpec as P


def shifted(shard, axis, by):
    count = lax.axis_size(axis)
    pairs = [(i, i + by) for i in range(count) if 0 <= i + by < count]
    return lax.ppermute(shard, axis, pairs)


def extended_2(block, sides, width):
    for axis, dim in sides:
        count = lax.axis_size(axis)
        forward = [(i, i + 1) for i in range(count - 1)]
        backward = [(target, source) for source, target in forward]
        low = lax.ppermute(
            lax.slice_in_dim(block, block.shape[dim] - width, None, axis=dim), axis, forward
        )
        high = lax.ppermute(lax.slice_in_dim(block, 0, width, axis=dim), axis, backward)
        block = jnp.concatenate([low, block, high], axis=dim)
    return block


def conv_valid(extended, kernel, bias):
    padded = jnp.pad(extended, ((0, 0), (0, 0), (0, 0), (0, 0), (1, 1)))
    result = lax.conv_general_dilated(
        padded,
        kernel,
        (1, 1, 1),
        "VALID",
        dimension_numbers=("NCDHW", "OIDHW", "NCDHW"),
        preferred_element_type=jnp.float32,
    )
    return result + bias[None, :, None, None, None]


def pixel_extend(pixels):
    earlier = shifted(pixels, "tm", 1)
    extended = jnp.concatenate([earlier, pixels], axis=2)
    return extended_2(extended, (("height", 3),), 1)


def feature_extend(act):
    earlier = shifted(act[:, :, -2:], "tm", 1)
    extended = jnp.concatenate([earlier, act], axis=2)
    return extended_2(extended, (("height", 3),), 1)


def encode(pixels, w_in, b_in, gain, w_mid, b_mid):
    stem = conv_valid(pixel_extend(pixels), w_in, b_in).astype(jnp.bfloat16)
    stem_wide = stem.astype(jnp.float32)
    scale_inv = lax.rsqrt(jnp.mean(stem_wide * stem_wide, axis=1, keepdims=True) + 1e-06)
    act = jax.nn.silu(stem_wide * scale_inv * gain[None, :, None, None, None]).astype(jnp.bfloat16)
    return (conv_valid(feature_extend(act), w_mid, b_mid) + stem_wide).astype(jnp.bfloat16)


def local(pixels, lengths, route, w_in, b_in, gain, w_mid, b_mid):
    groups = lax.axis_size("clip")
    my_clip = lax.axis_index("clip")
    route_grid = route.reshape(groups, -1)
    my_route = lax.dynamic_index_in_dim(route_grid, my_clip, 0, keepdims=False)
    send_order = jnp.argsort(my_route)
    arrived = lax.all_to_all(
        jnp.take(pixels, send_order, axis=0), "clip", split_axis=0, concat_axis=0, tiled=True
    )
    block = encode(arrived, w_in, b_in, gain, w_mid, b_mid)
    matches = route_grid == my_clip
    slot_length = jnp.sum(jnp.where(matches, lengths.reshape(groups, -1), 0), axis=1)
    frames_here = block.shape[2]
    frame_ids = lax.axis_index("tm") * frames_here + jnp.arange(frames_here, dtype=jnp.int32)
    keep = (frame_ids[None, :] < slot_length[:, None])[:, None, :, None, None]
    return jnp.where(keep, block, jnp.zeros_like(block))


def solution(mesh):
    placed = (P("clip", None, "tm", "height", None), P(), P(), P(), P(), P(), P(), P())
    return jax.shard_map(
        local,
        mesh=mesh,
        in_specs=placed,
        out_specs=P("clip", None, "tm", "height", None),
        check_vma=False,
    )
```

profile of v0, /device:TPU:0, one launch (start us, length us, event | category | flops | bytes accessed | tf_op | source)
XLA Modules:
  0.0 108.0 jit_solution(14934734676242115279)
XLA Ops:
  0.0 0.0 copy-start
  0.0 0.8 reshape.73
  0.8 0.7 sort.17
  1.6 1.3 %gather_fusion = bf16[4,3,2,384]{3,2,1,0:T(2,128)(2,1)S(1)} fusion(bf16[4,3,2,384]{3,2,1,0:T(2,128)(2,1)} %bitcast.43, s32[1024]{0:T(1024)S(1)} %pad_clamp_fusion), kind=kCustom, calls=%fused_computation | custom fusion | bytes 36880 | tf_op jit(solution)/shard_map/jit(_take)/gather | solution.py:66
  2.9 0.1 broadcast_select_fusion
  3.0 7.9 %all_to_all.5 = bf16[4,3,2,1,384]{4,2,1,3,0:T(2,128)(2,1)S(1)} all-to-all(bf16[4,3,2,1,384]{4,2,1,3,0:T(2,128)(2,1)S(1)} %broadcast_select_fusion), channel_id=1, replica_groups=mesh['clip'=4,'tm'=2,'height'=4] {'clip'}, dimensions={0} | all-to-all | bytes 36864 | tf_op jit(solution)/shard_map/all_to_all | solution.py:65
  10.9 3.4 %collective-permute-start = (bf16[4,3,2,1,384]{4,2,1,3,0:T(2,128)(2,1)S(1)}, bf16[4,3,2,1,384]{4,2,1,3,0:T(2,128)(2,1)S(1)}, u32[]{:S(2)}, u32[]{:S(2)}) collective-permute-start(bf16[4,3,2,1,384]{4,2,1,3,0:T(2,128)(2,1)S(1)} %all_to_all.5), channel_id=1, source_target_pairs={{0,4},{1,5},{2,6},{3,7},{8,12},{9,13},{10,14},{11,15},{16,20},{17,... | collective-permute-start | bytes 55304 | tf_op jit(solution)/shard_map/ppermute | solution.py:10
  14.3 1.4 %collective-permute-done = bf16[4,3,2,1,384]{4,2,1,3,0:T(2,128)(2,1)S(1)} collective-permute-done((bf16[4,3,2,1,384]{4,2,1,3,0:T(2,128)(2,1)S(1)}, bf16[4,3,2,1,384]{4,2,1,3,0:T(2,128)(2,1)S(1)}, u32[]{:S(2)}, u32[]{:S(2)}) %collective-permute-start) | collective-permute-done | bytes 18464 | tf_op jit(solution)/shard_map/ppermute | solution.py:10
  15.8 3.5 %collective-permute-start.1 = (bf16[4,3,4,1,384]{4,2,1,3,0:T(4,128)(2,1)S(1)}, bf16[4,3,4,1,384]{4,2,1,3,0:T(4,128)(2,1)S(1)}, u32[]{:S(2)}, u32[]{:S(2)}) collective-permute-start(bf16[4,3,4,1,384]{4,2,1,3,0:T(4,128)(2,1)S(1)} %pad_maximum_fusion.1), channel_id=1, source_target_pairs={{0,1},{1,2},{2,3},{4,5},{5,6},{6,7},{8,9},{9,10},{10,11},{12,13},{... | collective-permute-start | bytes 110600 | tf_op jit(solution)/shard_map/ppermute | solution.py:18
  19.3 1.3 %collective-permute-start.2 = (bf16[4,3,4,1,384]{4,2,1,3,0:T(4,128)(2,1)S(1)}, bf16[4,3,4,1,384]{4,2,1,3,0:T(4,128)(2,1)S(1)}, u32[]{:S(2)}, u32[]{:S(2)}) collective-permute-start(bf16[4,3,4,1,384]{4,2,1,3,0:T(4,128)(2,1)S(1)} %pad_maximum_fusion.1), channel_id=1, source_target_pairs={{1,0},{2,1},{3,2},{5,4},{6,5},{7,6},{9,8},{10,9},{11,10},{13,12},{... | collective-permute-start | bytes 110600 | tf_op jit(solution)/shard_map/ppermute | solution.py:21
  20.6 0.3 collective-permute-done.1
  20.9 4.2 %collective-permute-done.2 = bf16[4,3,4,1,384]{4,2,1,3,0:T(4,128)(2,1)S(1)} collective-permute-done((bf16[4,3,4,1,384]{4,2,1,3,0:T(4,128)(2,1)S(1)}, bf16[4,3,4,1,384]{4,2,1,3,0:T(4,128)(2,1)S(1)}, u32[]{:S(2)}, u32[]{:S(2)}) %collective-permute-start.2) | collective-permute-done | bytes 36896 | tf_op jit(solution)/shard_map/ppermute | solution.py:21
  25.1 0.1 maximum_bitcast_fusion.1
  25.2 0.0 copy-start.6
  25.2 0.0 copy-start.7
  25.2 0.0 copy-start.9
  25.3 0.1 pad.4.clone
  25.5 0.3 reshape.77
  25.8 0.1 slice.7
  25.8 0.2 fusion.13
  26.1 0.4 copy.50
  26.5 0.0 copy-done.6
  26.5 0.0 copy-done.7
  26.5 0.0 copy-done.9
  26.5 1.6 %multiply_reduce_fusion = (f32[2,32,49]{1,2,0:T(8,128)S(1)}, f32[2,1,32,49,96]{4,2,3,1,0:T(8,128)S(1)}) fusion(f32[96]{0:T(128)S(1)} %copy-done.7, bf16[3,4,3,32,51]{3,0,4,2,1:T(4,128)(2,1)S(1)} %copy.50, bf16[96,3,3,3,3]{0,4,3,2,1:T(4,128)(2,1)S(1)} %copy-done.6, pred[32,49]{0,1:T(8,128)(4,1)S(1)} %copy-done.9), kind=kOutput, calls=%fused_computation.9 | convolution fusion | flops 50574272 | bytes 1351776 | tf_op jit(solution)/shard_map/conv_general_dilated | solution.py:28
  28.2 0.0 copy-start.1
  28.2 1.2 %copy.52 = f32[2,1,32,49,96]{4,0,3,2,1:T(2,128)S(1)} copy(f32[2,1,32,49,96]{4,2,3,1,0:T(8,128)S(1)} %get-tuple-element.8) | data formatting | bytes 2408448 | tf_op jit(solution)/shard_map/convert_element_type | solution.py:53
  29.4 0.0 copy-done.1
  29.4 0.1 slice.8
  29.5 0.0 copy-start.5
  29.5 0.7 copy.61
  30.3 0.1 copy.54
  30.4 0.1 reshape.83
  30.5 0.0 copy-done.5
  30.5 0.5 multiply_convert_fusion
  31.0 0.0 copy-start.4
  31.0 4.2 %collective-permute-start.3 = (bf16[4,96,2,1,384]{4,1,3,2,0:T(8,128)(2,1)S(1)}, bf16[4,96,2,1,384]{4,1,3,2,0:T(8,128)(2,1)S(1)}, u32[]{:S(2)}, u32[]{:S(2)}) collective-permute-start(bf16[4,96,2,1,384]{4,1,3,2,0:T(8,128)(2,1)S(1)} %multiply_convert_fusion), channel_id=1, source_target_pairs={{0,4},{1,5},{2,6},{3,7},{8,12},{9,13},{10,14},{11,15},{16,20},{17,... | collective-permute-start | bytes 1769480 | tf_op jit(solution)/shard_map/ppermute | solution.py:10
  35.2 9.9 %collective-permute-done.3 = bf16[4,96,2,1,384]{4,1,3,2,0:T(8,128)(2,1)S(1)} collective-permute-done((bf16[4,96,2,1,384]{4,1,3,2,0:T(8,128)(2,1)S(1)}, bf16[4,96,2,1,384]{4,1,3,2,0:T(8,128)(2,1)S(1)}, u32[]{:S(2)}, u32[]{:S(2)}) %collective-permute-start.3) | collective-permute-done | bytes 589856 | tf_op jit(solution)/shard_map/ppermute | solution.py:10
  45.1 1.2 %pad_maximum_fusion = bf16[4,96,4,1,384]{4,1,3,2,0:T(8,128)(2,1)} fusion(bf16[4,96,2,1,384]{4,1,3,2,0:T(8,128)(2,1)S(1)} %multiply_convert_fusion, bf16[4,96,2,1,384]{4,1,3,2,0:T(8,128)(2,1)S(1)} %collective-permute-done.3), kind=kLoop, calls=%fused_computation.13 | loop fusion | flops 589824 | bytes 2359296 | tf_op jit(solution)/shard_map/concatenate | solution.py:47
  46.3 3.5 %collective-permute-start.4 = (bf16[4,96,4,1,384]{4,1,3,2,0:T(8,128)(2,1)}, bf16[4,96,4,1,384]{4,1,3,2,0:T(8,128)(2,1)S(1)}, u32[]{:S(2)}, u32[]{:S(2)}) collective-permute-start(bf16[4,96,4,1,384]{4,1,3,2,0:T(8,128)(2,1)} %pad_maximum_fusion), channel_id=1, source_target_pairs={{0,1},{1,2},{2,3},{4,5},{5,6},{6,7},{8,9},{9,10},{10,11},{12,13},{... | collective-permute-start | bytes 3538952 | tf_op jit(solution)/shard_map/ppermute | solution.py:18
  49.8 1.5 %collective-permute-start.5 = (bf16[4,96,4,1,384]{4,1,3,2,0:T(8,128)(2,1)}, bf16[4,96,4,1,384]{4,1,3,2,0:T(8,128)(2,1)}, u32[]{:S(2)}, u32[]{:S(2)}) collective-permute-start(bf16[4,96,4,1,384]{4,1,3,2,0:T(8,128)(2,1)} %pad_maximum_fusion), channel_id=1, source_target_pairs={{1,0},{2,1},{3,2},{5,4},{6,5},{7,6},{9,8},{10,9},{11,10},{13,12},{... | collective-permute-start | bytes 3538952 | tf_op jit(solution)/shard_map/ppermute | solution.py:21
  51.3 0.0 copy-done.4
  51.3 0.1 reshape.74
  51.4 0.1 select_reduce_fusion
  51.5 0.1 compare_bitcast_fusion
  51.6 0.2 broadcast.79
  51.8 1.0 reshape.89
  52.8 18.9 %collective-permute-done.4 = bf16[4,96,4,1,384]{4,1,3,2,0:T(8,128)(2,1)S(1)} collective-permute-done((bf16[4,96,4,1,384]{4,1,3,2,0:T(8,128)(2,1)}, bf16[4,96,4,1,384]{4,1,3,2,0:T(8,128)(2,1)S(1)}, u32[]{:S(2)}, u32[]{:S(2)}) %collective-permute-start.4) | collective-permute-done | bytes 1179680 | tf_op jit(solution)/shard_map/ppermute | solution.py:18
  71.7 4.2 %collective-permute-done.5 = bf16[4,96,4,1,384]{4,1,3,2,0:T(8,128)(2,1)} collective-permute-done((bf16[4,96,4,1,384]{4,1,3,2,0:T(8,128)(2,1)}, bf16[4,96,4,1,384]{4,1,3,2,0:T(8,128)(2,1)}, u32[]{:S(2)}, u32[]{:S(2)}) %collective-permute-start.5) | collective-permute-done | bytes 1179680 | tf_op jit(solution)/shard_map/ppermute | solution.py:21
  75.9 3.1 %maximum_bitcast_fusion = bf16[96,4,3,4,384]{4,0,2,1,3:T(8,128)(2,1)} fusion(bf16[4,96,4,1,384]{4,1,3,2,0:T(8,128)(2,1)} %collective-permute-done.5, bf16[4,96,2,1,384]{4,1,3,2,0:T(8,128)(2,1)S(1)} %multiply_convert_fusion, bf16[4,96,2,1,384]{4,1,3,2,0:T(8,128)(2,1)S(1)} %collective-permute-done.3, bf16[4,96,4,1,384]{4,1,3,2,0:T(8,128)(2,1)S(1)} %collective-permute-done.4), kind=kLoop, calls=%fused_computation.7 | loop fusion | flops 5308416 | bytes 7077888 | tf_op jit(solution)/shard_map/concatenate | solution.py:22
  79.0 8.0 %copy.63 = bf16[96,4,3,4,384]{0,3,4,2,1:T(4,128)(2,1)} copy(bf16[96,4,3,4,384]{4,0,2,1,3:T(8,128)(2,1)} %maximum_bitcast_fusion) | data formatting | bytes 7077888
  87.0 4.8 %pad.6.clone = bf16[96,4,3,4,392]{0,3,4,2,1:T(4,128)(2,1)S(1)} pad(bf16[96,4,3,4,384]{0,3,4,2,1:T(4,128)(2,1)} %copy.63, bf16[]{:T(256)} %constant.45.clone.1), padding=0_0x0_0x0_0x0_0x1_7 | pad | bytes 7151618 | tf_op jit(solution)/shard_map/concatenate | solution.py:22
  91.8 0.1 slice.10
  91.9 0.0 copy-start.2
  91.9 0.0 copy-start.3
  91.9 0.0 copy-start.8
  91.9 4.9 %fusion.1 = bf16[96,4,3,4,8,51]{0,3,5,4,2,1:T(4,128)(2,1)} fusion(bf16[96,4,3,4,7,2]{0,3,5,4,2,1:T(4,128)(2,1)S(1)} %slice.10, bf16[96,4,3,4,8,49]{0,3,5,4,2,1:T(4,128)(2,1)S(1)} %bitcast.40), kind=kLoop, calls=%fused_computation.3 | loop fusion | flops 11280384 | bytes 7501824 | tf_op jit(solution)/shard_map/conv_general_dilated | solution.py:28
  96.9 0.0 copy-done
  96.9 0.0 copy-done.2
  96.9 0.0 copy-done.8
  96.9 8.1 %copy_select_fusion = bf16[2,1,32,49,96]{4,2,3,1,0:T(8,128)(2,1)S(1)} fusion(pred[2,1,32,49,96]{4,3,2,0,1:T(8,128)(4,1)S(1)} %copy-done.3, f32[2,1,32,49,96]{4,2,3,1,0:T(8,128)S(1)} %copy-done.2, bf16[96,96,3,3,3]{1,0,4,3,2:T(8,128)(2,1)S(1)} %copy-done, bf16[96,4,3,4,8,51]{0,3,5,4,2,1:T(4,128)(2,1)} %fusion.1, f32[96]{0:T(128)S(1)} %copy-done.8, ...), kind=kOutput, calls=%fused_computation.11 | convolution fusion | flops 1562179584 | bytes 6367136 | tf_op jit(solution)/shard_map/conv_general_dilated | solution.py:28
  105.0 0.6 copy.59
  105.6 0.5 slice_bitcast_fusion
  106.2 1.9 %copy.60 = bf16[4,96,2,1,384]{4,2,3,1,0:T(2,128)(2,1)} copy(bf16[4,96,2,1,384]{1,2,4,0,3:T(2,128)(2,1)S(1)} %slice_bitcast_fusion) | data formatting | bytes 1179648 | tf_op jit(solution)/shard_map/jit(_where)/select_n | solution.py:74
  (12 shorter events, 0.1 us)
Async XLA Ops:
  0.0 96.9 %copy-start = (bf16[96,96,3,3,3]{1,0,4,3,2:T(8,128)(2,1)S(1)}, bf16[96,96,3,3,3]{1,0,4,3,2:T(8,128)(2,1)}, u32[]{:S(2)}) copy-start(bf16[96,96,3,3,3]{1,0,4,3,2:T(8,128)(2,1)} %param.14) | copy-start | bytes 1492996
  10.9 4.8 %collective-permute-start = (bf16[4,3,2,1,384]{4,2,1,3,0:T(2,128)(2,1)S(1)}, bf16[4,3,2,1,384]{4,2,1,3,0:T(2,128)(2,1)S(1)}, u32[]{:S(2)}, u32[]{:S(2)}) collective-permute-start(bf16[4,3,2,1,384]{4,2,1,3,0:T(2,128)(2,1)S(1)} %all_to_all.5), channel_id=1, source_target_pairs={{0,4},{1,5},{2,6},{3,7},{8,12},{9,13},{10,14},{11,15},{16,20},{17,... | collective-permute-start | bytes 55304 | tf_op jit(solution)/shard_map/ppermute | solution.py:10
  15.8 5.1 %collective-permute-start.1 = (bf16[4,3,4,1,384]{4,2,1,3,0:T(4,128)(2,1)S(1)}, bf16[4,3,4,1,384]{4,2,1,3,0:T(4,128)(2,1)S(1)}, u32[]{:S(2)}, u32[]{:S(2)}) collective-permute-start(bf16[4,3,4,1,384]{4,2,1,3,0:T(4,128)(2,1)S(1)} %pad_maximum_fusion.1), channel_id=1, source_target_pairs={{0,1},{1,2},{2,3},{4,5},{5,6},{6,7},{8,9},{9,10},{10,11},{12,13},{... | collective-permute-start | bytes 110600 | tf_op jit(solution)/shard_map/ppermute | solution.py:18
  19.3 5.9 %collective-permute-start.2 = (bf16[4,3,4,1,384]{4,2,1,3,0:T(4,128)(2,1)S(1)}, bf16[4,3,4,1,384]{4,2,1,3,0:T(4,128)(2,1)S(1)}, u32[]{:S(2)}, u32[]{:S(2)}) collective-permute-start(bf16[4,3,4,1,384]{4,2,1,3,0:T(4,128)(2,1)S(1)} %pad_maximum_fusion.1), channel_id=1, source_target_pairs={{1,0},{2,1},{3,2},{5,4},{6,5},{7,6},{9,8},{10,9},{11,10},{13,12},{... | collective-permute-start | bytes 110600 | tf_op jit(solution)/shard_map/ppermute | solution.py:21
  25.2 1.3 %copy-start.6 = (bf16[96,3,3,3,3]{0,4,3,2,1:T(4,128)(2,1)S(1)}, bf16[96,3,3,3,3]{0,4,3,2,1:T(4,128)(2,1)}, u32[]{:S(2)}) copy-start(bf16[96,3,3,3,3]{0,4,3,2,1:T(4,128)(2,1)} %param.11) | copy-start | bytes 46660
  25.2 1.3 %copy-start.7 = (f32[96]{0:T(128)S(1)}, f32[96]{0:T(128)}, u32[]{:S(2)}) copy-start(f32[96]{0:T(128)} %param.12) | copy-start | bytes 1156
  25.2 1.3 %copy-start.9 = (pred[32,49]{0,1:T(8,128)(4,1)S(1)}, pred[32,49]{0,1:T(8,128)(4,1)}, u32[]{:S(2)}) copy-start(pred[32,49]{0,1:T(8,128)(4,1)} %constant.55) | copy-start | bytes 4708
  28.2 1.3 %copy-start.1 = (f32[2,1,32,49,96]{4,2,3,1,0:T(8,128)}, f32[2,1,32,49,96]{4,2,3,1,0:T(8,128)S(1)}, u32[]{:S(2)}) copy-start(f32[2,1,32,49,96]{4,2,3,1,0:T(8,128)S(1)} %get-tuple-element.8) | copy-start | bytes 3612676
  29.5 0.9 copy-start.5
  31.0 20.4 %copy-start.4 = (s32[16]{0:T(128)S(1)}, s32[16]{0:T(128)}, u32[]{:S(2)}) copy-start(s32[16]{0:T(128)} %param.9) | copy-start | bytes 196
  31.0 14.1 %collective-permute-start.3 = (bf16[4,96,2,1,384]{4,1,3,2,0:T(8,128)(2,1)S(1)}, bf16[4,96,2,1,384]{4,1,3,2,0:T(8,128)(2,1)S(1)}, u32[]{:S(2)}, u32[]{:S(2)}) collective-permute-start(bf16[4,96,2,1,384]{4,1,3,2,0:T(8,128)(2,1)S(1)} %multiply_convert_fusion), channel_id=1, source_target_pairs={{0,4},{1,5},{2,6},{3,7},{8,12},{9,13},{10,14},{11,15},{16,20},{17,... | collective-permute-start | bytes 1769480 | tf_op jit(solution)/shard_map/ppermute | solution.py:10
  46.3 25.4 %collective-permute-start.4 = (bf16[4,96,4,1,384]{4,1,3,2,0:T(8,128)(2,1)}, bf16[4,96,4,1,384]{4,1,3,2,0:T(8,128)(2,1)S(1)}, u32[]{:S(2)}, u32[]{:S(2)}) collective-permute-start(bf16[4,96,4,1,384]{4,1,3,2,0:T(8,128)(2,1)} %pad_maximum_fusion), channel_id=1, source_target_pairs={{0,1},{1,2},{2,3},{4,5},{5,6},{6,7},{8,9},{9,10},{10,11},{12,13},{... | collective-permute-start | bytes 3538952 | tf_op jit(solution)/shard_map/ppermute | solution.py:18
  49.8 26.1 %collective-permute-start.5 = (bf16[4,96,4,1,384]{4,1,3,2,0:T(8,128)(2,1)}, bf16[4,96,4,1,384]{4,1,3,2,0:T(8,128)(2,1)}, u32[]{:S(2)}, u32[]{:S(2)}) collective-permute-start(bf16[4,96,4,1,384]{4,1,3,2,0:T(8,128)(2,1)} %pad_maximum_fusion), channel_id=1, source_target_pairs={{1,0},{2,1},{3,2},{5,4},{6,5},{7,6},{9,8},{10,9},{11,10},{13,12},{... | collective-permute-start | bytes 3538952 | tf_op jit(solution)/shard_map/ppermute | solution.py:21
  91.9 5.0 %copy-start.2 = (f32[2,1,32,49,96]{4,2,3,1,0:T(8,128)S(1)}, f32[2,1,32,49,96]{4,2,3,1,0:T(8,128)}, u32[]{:S(2)}) copy-start(f32[2,1,32,49,96]{4,2,3,1,0:T(8,128)} %copy-done.1) | copy-start | bytes 3612676
  91.9 5.0 %copy-start.3 = (pred[2,1,32,49,96]{4,3,2,0,1:T(8,128)(4,1)S(1)}, pred[2,1,32,49,96]{4,3,2,0,1:T(8,128)(4,1)}, u32[]{:S(2)}) copy-start(pred[2,1,32,49,96]{4,3,2,0,1:T(8,128)(4,1)} %reshape.89) | copy-start | bytes 903172
  91.9 5.0 %copy-start.8 = (f32[96]{0:T(128)S(1)}, f32[96]{0:T(128)}, u32[]{:S(2)}) copy-start(f32[96]{0:T(128)} %param.15) | copy-start | bytes 1156
where the time goes:
time: 109 us; the launch traced here: 108 us
  waiting for transfers between devices  39 us (36%)
  local copies, waits for them, and re-layouts  22.6 us (21%)
  starting transfers between devices  17.4 us (16%)
  other arithmetic  11.1 us (10%)
  matrix products  9.71 us (9%)
  blocking collectives  7.91 us (7%)
    ppermute x2, waiting for transfers between devices, extended_2(): lax.ppermute(lax.slice_in_dim(block, block.shape[dim] - width, None, axis...  19.2 us
    ppermute x2, waiting for transfers between devices, shifted(): return lax.ppermute(shard, axis, pairs)  11.3 us
    conv_general_dilated x2, matrix products, conv_valid(): lax.conv_general_dilated(padded, kernel, (1, 1, 1), 'VALID', dimension_nu...  9.71 us
    unnamed x24, local copies, waits for them, and re-layouts  8.94 us
    ppermute x2, waiting for transfers between devices, extended_2(): lax.ppermute(lax.slice_in_dim(block, 0, width, axis=dim), axis, backward)  8.42 us
    all_to_all x1, blocking collectives, local(): lax.all_to_all(jnp.take(pixels, send_order, axis=0), 'clip', split_axis=0...  7.91 us
    ppermute x2, starting transfers between devices, shifted(): return lax.ppermute(shard, axis, pairs)  7.62 us
    ppermute x2, starting transfers between devices, extended_2(): lax.ppermute(lax.slice_in_dim(block, block.shape[dim] - width, None, axis...  7.03 us
  transfers between devices with their start and end apart: 6, of which 6 were waited for; matrix products, arithmetic and copies ran while one was open for 1% of the time, Pallas kernels for 0%

commit v1 on v0

v1 whole, which is shorter than its diff:
```python
import functools

import jax
import jax.numpy as jnp
from jax import lax
from jax.experimental import pallas as pl
from jax.experimental.pallas import tpu as pltpu
from jax.sharding import PartitionSpec as P

F32, BF16 = jnp.float32, jnp.bfloat16
REACH = (-2, -1, 1, 2)


def gather_kernel(groups, heights, route_ref, pix_ref, out_ref, send, s1, r1, s2, r2):
    clip = lax.axis_index("clip")
    tm = lax.axis_index("tm")
    h = lax.axis_index("height")

    def there(dz):
        return jnp.logical_and(h + dz >= 0, h + dz < heights)

    barrier = pltpu.get_barrier_semaphore()
    for k in range(1, groups):
        pl.semaphore_signal(barrier, inc=1, device_id={"clip": lax.rem(clip + k, groups)})
    pl.semaphore_signal(barrier, inc=1, device_id={"tm": 1 - tm})
    count = groups
    for dz in REACH:
        @pl.when(there(dz))
        def _(dz=dz):
            pl.semaphore_signal(barrier, inc=1, device_id={"height": h + dz})
            pl.semaphore_signal(barrier, inc=1, device_id={"tm": 1 - tm, "height": h + dz})
        count = count + 2 * there(dz).astype(jnp.int32)

    for d in range(groups):
        total = None
        for j in range(groups):
            hit = (route_ref[clip * groups + j] == d).astype(F32)
            term = pix_ref[j].astype(F32) * hit
            total = term if total is None else total + term
        send[d] = total.astype(BF16)
    out_ref[1, 2, clip] = send[clip]
    zero = jnp.zeros(out_ref.shape[2:], BF16)
    for k in range(5):
        lost = jnp.logical_not(there(k - 2))

        @pl.when(jnp.logical_or(lost, tm == 0))
        def _(k=k):
            out_ref[0, k] = zero
        if k != 2:
            @pl.when(lost)
            def _(k=k):
                out_ref[1, k] = zero

    pl.semaphore_wait(barrier, count)
    first = []
    for k in range(1, groups):
        d = lax.rem(clip + k, groups)
        copy = pltpu.make_async_remote_copy(
            send.at[d], out_ref.at[1, 2, clip], s1.at[k], r1.at[k],
            device_id={"clip": d})
        copy.start()
        first.append(copy)
    for k in range(1, groups):
        source = lax.rem(clip + groups - k, groups)
        pltpu.make_async_remote_copy(
            send.at[0], out_ref.at[1, 2, source], s1.at[k], r1.at[k],
            device_id={"clip": source}).wait_recv()

    def out_going(j, dz):
        place = {"height": h + dz} if j == 1 else {"tm": 1 - tm, "height": h + dz}
        return pltpu.make_async_remote_copy(
            out_ref.at[1, 2], out_ref.at[j, 2 - dz], s2.at[j, 2 - dz], r2.at[j, 2 - dz],
            device_id=place)

    def in_coming(j, k):
        return pltpu.make_async_remote_copy(
            out_ref.at[1, 2], out_ref.at[j, k], s2.at[j, k], r2.at[j, k],
            device_id={"tm": 1 - tm})

    hops = [(0, 0)] + [(j, dz) for dz in (1, -1, 2, -2) for j in (0, 1)]
    for j, dz in hops:
        @pl.when(jnp.logical_and(there(dz), jnp.logical_or(j == 1, tm == 0)))
        def _(j=j, dz=dz):
            out_going(j, dz).start()
    for copy in first:
        copy.wait_send()
    for j, dz in hops:
        @pl.when(jnp.logical_and(there(dz), jnp.logical_or(j == 1, tm == 1)))
        def _(j=j, dz=dz):
            in_coming(j, 2 + dz).wait_recv()
    for j, dz in hops:
        @pl.when(jnp.logical_and(there(dz), jnp.logical_or(j == 1, tm == 0)))
        def _(j=j, dz=dz):
            out_going(j, dz).wait_send()


def encode_kernel(groups, heights, lengths_ref, route_ref, pix_ref, w1_ref, par_ref, w2_ref, out_ref, grid, cols, acts, wide):
    ch = par_ref.shape[0]
    width = pix_ref.shape[-1]
    clip = lax.axis_index("clip")
    tm = lax.axis_index("tm")
    h = lax.axis_index("height")
    lane = lax.broadcasted_iota(jnp.int32, (1, width), 1)
    b_in = par_ref[:, 0:1]
    gain = par_ref[:, 1:2]
    b_mid = par_ref[:, 2:3]

    def right(v):
        return jnp.where(lane == 0, 0.0, pltpu.roll(v, 1, 1))

    def left(v):
        return jnp.where(lane == width - 1, 0.0, pltpu.roll(v, width - 1, 1))

    wide[...] = jnp.zeros_like(wide)
    for dt in range(3):
        for dr in range(3):
            for dc in range(3):
                at = (dt * 3 + dr) * 128
                wide[dc * ch:(dc + 1) * ch, at:at + ch] = w2_ref[dt, dr, dc]

    def one(c, carry):
        grid[...] = jnp.zeros_like(grid)
        for j in range(2):
            for k in range(5):
                for f in range(2):
                    grid[2 + 2 * j + f, 3 * k:3 * k + 3, :] = pix_ref[j, k, c, f].astype(F32)
        for p in range(6):
            v = grid[p]
            cols[p * 48:p * 48 + 16, :] = right(v).astype(BF16)
            cols[p * 48 + 16:p * 48 + 32, :] = v.astype(BF16)
            cols[p * 48 + 32:p * 48 + 48, :] = left(v).astype(BF16)
        kept = []
        pad = jnp.zeros((128 - ch, width), BF16)
        for f in range(4):
            s = jnp.dot(w1_ref[...], cols[f * 48:f * 48 + 144, :], preferred_element_type=F32)
            for r in range(3):
                stem = (s[r * ch:(r + 1) * ch] + b_in).astype(BF16).astype(F32)
                scale = lax.rsqrt(jnp.mean(stem * stem, axis=0, keepdims=True) + 1e-6)
                v = 0.5 * (stem * scale * gain)
                act = v + v * jnp.tanh(v)
                live = jnp.logical_and(h - 1 + r >= 0, h - 1 + r < heights)
                if f < 2:
                    live = jnp.logical_and(live, tm > 0)
                at = (f * 3 + r) * 128
                acts[at:at + ch, :] = jnp.where(live, act, 0.0).astype(BF16)
                acts[at + ch:at + 128, :] = pad
                if f >= 2 and r == 1:
                    kept.append(stem)
        length = 0
        for j in range(groups):
            q = c * groups + j
            length = length + jnp.where(route_ref[q] == clip, lengths_ref[q], 0)
        for t in range(2):
            y = jnp.dot(wide[...], acts[t * 384:t * 384 + 1152, :], preferred_element_type=F32)
            o = y[ch:2 * ch] + right(y[:ch]) + left(y[2 * ch:]) + b_mid + kept[t]
            out_ref[c, t] = jnp.where(tm * 2 + t < length, o, 0.0).astype(BF16)
        return carry

    lax.fori_loop(0, groups, one, 0)


def local(groups, heights, pixels, lengths, route, w_in, b_in, gain, w_mid, b_mid):
    clips, colours, frames, _, width = pixels.shape
    ch = w_in.shape[0]
    vmem = pl.BlockSpec(memory_space=pltpu.VMEM)
    smem = pl.BlockSpec(memory_space=pltpu.SMEM)
    pix = jnp.transpose(pixels[:, :, :, 0, :], (0, 2, 1, 3))
    around = pl.pallas_call(
        functools.partial(gather_kernel, groups, heights),
        out_shape=jax.ShapeDtypeStruct((2, 5, clips, frames, colours, width), BF16),
        in_specs=[smem, vmem],
        out_specs=vmem,
        scratch_shapes=[
            pltpu.VMEM((groups, frames, colours, width), BF16),
            pltpu.SemaphoreType.DMA((groups,)),
            pltpu.SemaphoreType.DMA((groups,)),
            pltpu.SemaphoreType.DMA((2, 5)),
            pltpu.SemaphoreType.DMA((2, 5)),
        ],
        compiler_params=pltpu.CompilerParams(collective_id=0, has_side_effects=True),
    )(route, pix)
    taps = jnp.transpose(w_in, (0, 2, 4, 3, 1)).reshape(ch, 3, 3, 9)
    w1 = jnp.concatenate(
        [jnp.pad(taps, ((0, 0), (0, 0), (0, 0), (3 * r, 7 - 3 * r))).reshape(ch, 144) for r in range(3)], axis=0)
    par = jnp.stack([b_in, gain, b_mid], axis=1)
    w2 = jnp.transpose(w_mid, (2, 3, 4, 0, 1))
    out = pl.pallas_call(
        functools.partial(encode_kernel, groups, heights),
        out_shape=jax.ShapeDtypeStruct((clips, frames, ch, width), BF16),
        in_specs=[smem, smem, vmem, vmem, vmem, vmem],
        out_specs=vmem,
        scratch_shapes=[
            pltpu.VMEM((6, 16, width), F32),
            pltpu.VMEM((288, width), BF16),
            pltpu.VMEM((12 * 128, width), BF16),
            pltpu.VMEM((3 * ch, 9 * 128), BF16),
        ],
        compiler_params=pltpu.CompilerParams(vmem_limit_bytes=32 * 1024 * 1024),
    )(lengths, route, around, w1, par, w2)
    return jnp.transpose(out, (0, 2, 1, 3))[:, :, :, None, :]


def solution(mesh):
    placed = (P("clip", None, "tm", "height", None), P(), P(), P(), P(), P(), P(), P())
    return jax.shard_map(
        functools.partial(local, mesh.shape["clip"], mesh.shape["height"]),
        mesh=mesh,
        in_specs=placed,
        out_specs=P("clip", None, "tm", "height", None),
        check_vma=False,
    )
```

time: 109 us -> 29.5 us (0.27)
  waiting for transfers between devices: 39 us -> 0 us
  Pallas kernels: 0 us -> 23.6 us
  local copies, waits for them, and re-layouts: 22.6 us -> 4.75 us
  starting transfers between devices: 17.4 us -> 0 us
  other arithmetic: 11.1 us -> 0.79 us
  matrix products: 9.71 us -> 0 us
  blocking collectives: 7.91 us -> 0 us
    ppermute x6 -> x0, waiting for transfers between devices: 39 us -> none  [the longest x2 19.2 us: extended_2(): lax.ppermute(lax.slice_in_dim(block, block.shape[dim] - width, None, axis...]
    pallas_call x0 -> x2, Pallas kernels: none -> 23.6 us  [the longest x1 15.6 us: local(): pl.pallas_call(functools.partial(gather_kernel, groups, heights), out_sha...]
    ppermute x6 -> x0, starting transfers between devices: 17.4 us -> none  [the longest x2 7.62 us: shifted(): return lax.ppermute(shard, axis, pairs)]
    conv_general_dilated x2 -> x0, matrix products: 9.71 us -> none  [conv_valid(): lax.conv_general_dilated(padded, kernel, (1, 1, 1), 'VALID', dimension_nu...]
    all_to_all x1 -> x0, blocking collectives: 7.91 us -> none  [local(): lax.all_to_all(jnp.take(pixels, send_order, axis=0), 'clip', split_axis=0...]
    unnamed x24 -> x10, local copies, waits for them, and re-layouts: 8.94 us -> 2.3 us
    conv_general_dilated x2 -> x0, other arithmetic: 5.15 us -> none  [conv_valid(): lax.conv_general_dilated(padded, kernel, (1, 1, 1), 'VALID', dimension_nu...]
    concatenate x2 -> x0, local copies, waits for them, and re-layouts: 4.93 us -> none  [extended_2(): block = jnp.concatenate([low, block, high], axis=dim)]
  transfers between devices with their start and end apart: 6 -> 0, of which waited for: 6 -> 0; matrix products, arithmetic and copies ran while one was open for 1% -> 0% of each run, Pallas kernels for 0% -> 0%
where the time goes in v1:
time: 29.5 us; the launch traced here: 29.2 us
  Pallas kernels  23.6 us (80%)
  local copies, waits for them, and re-layouts  4.75 us (16%)
  other arithmetic  0.79 us (3%)
    pallas_call x1, Pallas kernels, local(): pl.pallas_call(functools.partial(gather_kernel, groups, heights), out_sha...  15.6 us
    pallas_call x1, Pallas kernels, local(): pl.pallas_call(functools.partial(encode_kernel, groups, heights), out_sha...  7.97 us
    unnamed x10, local copies, waits for them, and re-layouts  2.3 us
    broadcast_in_dim x1, local copies, waits for them, and re-layouts, local(): return jnp.transpose(out, (0, 2, 1, 3))[:, :, :, None, :]  1.27 us
    another operation x1, other arithmetic, local(): par = jnp.stack([b_in, gain, b_mid], axis=1)  0.76 us
    transpose x1, local copies, waits for them, and re-layouts, local(): taps = jnp.transpose(w_in, (0, 2, 4, 3, 1)).reshape(ch, 3, 3, 9)  0.76 us

profile of v1, /device:TPU:0, one launch (start us, length us, event | category | flops | bytes accessed | tf_op | source)
XLA Modules:
  0.0 29.2 jit_solution(41560941483828358)
XLA Ops:
  0.0 0.0 copy-start.1
  0.0 0.8 %pad_maximum_fusion.1 = f32[96,3]{0,1:T(4,128)S(1)} fusion(f32[96,1]{0,1:T(1,128)} %bitcast.25, f32[96,1]{0,1:T(1,128)} %bitcast.26, f32[96,1]{0,1:T(1,128)} %bitcast.27), kind=kLoop, calls=%fused_computation.2 | loop fusion | flops 576 | bytes 2304 | tf_op jit(solution)/shard_map/stack | solution.py:185
  0.8 1.3 %copy.40 = bf16[4,3,2,1,384]{4,1,2,0,3:T(4,128)(2,1)} copy(bf16[4,3,2,1,384]{4,2,3,1,0:T(2,128)(2,1)} %param.8) | data formatting | bytes 36864 | tf_op args[0]
  2.1 0.8 %copy.27 = bf16[96,3,3,3,3]{0,2,4,3,1:T(4,128)(2,1)S(1)} copy(bf16[96,3,3,3,3]{0,2,3,1,4:T(4,128)(2,1)} %bitcast.24) | data formatting | bytes 31104 | tf_op jit(solution)/shard_map/transpose | solution.py:182
  2.9 0.1 copy.34.par_ref
  3.0 0.1 copy.33
  3.1 0.1 copy.31
  3.2 0.1 copy.32
  3.4 0.0 copy-start.2
  3.4 0.0 copy-start.3
  3.4 15.6 %shard_map.82.pix_ref = bf16[2,5,4,2,3,384]{5,4,3,2,1,0:T(4,128)(2,1)} custom-call(s32[16]{0:T(128)} %route_ref.3, bf16[4,2,3,384]{3,2,1,0:T(4,128)(2,1)} %bitcast.23), custom_call_target="tpu_custom_call" | custom-call | tf_op jit(solution)/shard_map/pallas_call | solution.py:168
  19.0 0.0 copy-done.1
  19.0 0.0 copy-done.2
  19.0 0.0 copy-done.3
  19.0 0.0 copy-start
  19.0 0.9 %copy-done = bf16[2,5,4,2,3,384]{5,4,3,2,1,0:T(4,128)(2,1)S(1)} copy-done((bf16[2,5,4,2,3,384]{5,4,3,2,1,0:T(4,128)(2,1)S(1)}, bf16[2,5,4,2,3,384]{5,4,3,2,1,0:T(4,128)(2,1)}, u32[]{:S(2)}) %copy-start) | copy-done | bytes 184344
  20.0 8.0 %shard_map.83 = bf16[4,2,96,384]{3,2,1,0:T(8,128)(2,1)S(1)} custom-call(s32[16]{0:T(128)S(1)} %copy-done.3, s32[16]{0:T(128)S(1)} %copy-done.2, bf16[2,5,4,2,3,384]{5,4,3,2,1,0:T(4,128)(2,1)S(1)} %copy-done, bf16[288,144]{1,0:T(8,128)(2,1)S(1)} %pad_maximum_fusion.w1_ref, f32[96,3]{1,0:T(8,128)S(1)} %copy.34.par_ref, bf16[3,3,3,96,96]{4,3,2,1,0:T(8,128)(2,1)S(1)} %bitcast.18), custom_call_target="tpu_custom_call" | custom-call | tf_op jit(solution)/shard_map/pallas_call | solution.py:187
  27.9 1.3 %copy.35 = bf16[4,96,2,1,384]{4,2,3,1,0:T(2,128)(2,1)} copy(bf16[4,96,2,1,384]{4,1,2,0,3:T(8,128)(2,1)S(1)} %bitcast.17) | data formatting | bytes 1179648 | tf_op jit(solution)/shard_map/broadcast_in_dim | solution.py:200
  (3 shorter events, 0.1 us)
Async XLA Ops:
  0.0 19.0 %copy-start.1 = (bf16[96,96,3,3,3]{1,0,4,3,2:T(8,128)(2,1)S(1)}, bf16[96,96,3,3,3]{1,0,4,3,2:T(8,128)(2,1)}, u32[]{:S(2)}) copy-start(bf16[96,96,3,3,3]{1,0,4,3,2:T(8,128)(2,1)} %param.14) | copy-start | bytes 1492996
  3.4 15.6 %copy-start.2 = (s32[16]{0:T(128)S(1)}, s32[16]{0:T(128)}, u32[]{:S(2)}) copy-start(s32[16]{0:T(128)} %route_ref.3) | copy-start | bytes 196
  3.4 15.6 %copy-start.3 = (s32[16]{0:T(128)S(1)}, s32[16]{0:T(128)}, u32[]{:S(2)}) copy-start(s32[16]{0:T(128)} %lengths_ref.1) | copy-start | bytes 196
  19.0 0.9 %copy-start = (bf16[2,5,4,2,3,384]{5,4,3,2,1,0:T(4,128)(2,1)S(1)}, bf16[2,5,4,2,3,384]{5,4,3,2,1,0:T(4,128)(2,1)}, u32[]{:S(2)}) copy-start(bf16[2,5,4,2,3,384]{5,4,3,2,1,0:T(4,128)(2,1)} %shard_map.82.pix_ref) | copy-start | bytes 552964

commit v2 on v1

--- a/solution.py
+++ b/solution.py
@@ -37,7 +37,8 @@
             hit = (route_ref[clip * groups + j] == d).astype(F32)
             term = pix_ref[j].astype(F32) * hit
             total = term if total is None else total + term
-        send[d] = total.astype(BF16)
+        for f in range(total.shape[1]):
+            send[d, f] = total[:, f, :].astype(BF16)
     out_ref[1, 2, clip] = send[clip]
     zero = jnp.zeros(out_ref.shape[2:], BF16)
     for k in range(5):
@@ -94,16 +95,19 @@
             out_going(j, dz).wait_send()
 
 
-def encode_kernel(groups, heights, lengths_ref, route_ref, pix_ref, w1_ref, par_ref, w2_ref, out_ref, grid, cols, acts, wide):
-    ch = par_ref.shape[0]
+def encode_kernel(groups, heights, lengths_ref, route_ref, pix_ref, taps_ref, b_in_ref, gain_ref, b_mid_ref, w2_ref, out_ref,
+                  grid, cols, acts, wide, tall, w1_ref, rows):
+    ch = b_in_ref.shape[1]
     width = pix_ref.shape[-1]
     clip = lax.axis_index("clip")
     tm = lax.axis_index("tm")
     h = lax.axis_index("height")
     lane = lax.broadcasted_iota(jnp.int32, (1, width), 1)
-    b_in = par_ref[:, 0:1]
-    gain = par_ref[:, 1:2]
-    b_mid = par_ref[:, 2:3]
+    rows[...] = jnp.zeros_like(rows)
+    for n, row in enumerate((b_in_ref, gain_ref, b_mid_ref)):
+        rows[n:n + 1, :ch] = row[...]
+    par = rows[...].T[:ch]
+    b_in, gain, b_mid = par[:, 0:1], par[:, 1:2], par[:, 2:3]
 
     def right(v):
         return jnp.where(lane == 0, 0.0, pltpu.roll(v, 1, 1))
@@ -111,6 +115,17 @@
     def left(v):
         return jnp.where(lane == width - 1, 0.0, pltpu.roll(v, width - 1, 1))
 
+    tall[...] = jnp.zeros_like(tall)
+    for i in range(3):
+        for dt in range(3):
+            for dr in range(3):
+                piece = taps_ref[i, dt, dr].astype(F32)
+                for r in range(3):
+                    for dc in range(3):
+                        at = dt * 48 + dc * 16 + (r + dr) * 3 + i
+                        tall[at:at + 1, r * 128:r * 128 + ch] = piece[dc:dc + 1]
+    for r in range(3):
+        w1_ref[r * ch:(r + 1) * ch, :] = tall[:, r * 128:(r + 1) * 128].T[:ch].astype(BF16)
     wide[...] = jnp.zeros_like(wide)
     for dt in range(3):
         for dr in range(3):
@@ -164,7 +179,7 @@
     ch = w_in.shape[0]
     vmem = pl.BlockSpec(memory_space=pltpu.VMEM)
     smem = pl.BlockSpec(memory_space=pltpu.SMEM)
-    pix = jnp.transpose(pixels[:, :, :, 0, :], (0, 2, 1, 3))
+    pix = pixels.reshape(clips, colours, frames, width)
     around = pl.pallas_call(
         functools.partial(gather_kernel, groups, heights),
         out_shape=jax.ShapeDtypeStruct((2, 5, clips, frames, colours, width), BF16),
@@ -179,24 +194,25 @@
         ],
         compiler_params=pltpu.CompilerParams(collective_id=0, has_side_effects=True),
     )(route, pix)
-    taps = jnp.transpose(w_in, (0, 2, 4, 3, 1)).reshape(ch, 3, 3, 9)
-    w1 = jnp.concatenate(
-        [jnp.pad(taps, ((0, 0), (0, 0), (0, 0), (3 * r, 7 - 3 * r))).reshape(ch, 144) for r in range(3)], axis=0)
-    par = jnp.stack([b_in, gain, b_mid], axis=1)
+    w1 = jnp.transpose(w_in, (1, 2, 3, 4, 0))
+    rows = [v.reshape(1, ch) for v in (b_in, gain, b_mid)]
     w2 = jnp.transpose(w_mid, (2, 3, 4, 0, 1))
     out = pl.pallas_call(
         functools.partial(encode_kernel, groups, heights),
         out_shape=jax.ShapeDtypeStruct((clips, frames, ch, width), BF16),
-        in_specs=[smem, smem, vmem, vmem, vmem, vmem],
+        in_specs=[smem, smem] + [vmem] * 6,
         out_specs=vmem,
         scratch_shapes=[
             pltpu.VMEM((6, 16, width), F32),
             pltpu.VMEM((288, width), BF16),
             pltpu.VMEM((12 * 128, width), BF16),
             pltpu.VMEM((3 * ch, 9 * 128), BF16),
+            pltpu.VMEM((144, 3 * 128), F32),
+            pltpu.VMEM((3 * ch, 144), BF16),
+            pltpu.VMEM((8, 128), F32),
         ],
         compiler_params=pltpu.CompilerParams(vmem_limit_bytes=32 * 1024 * 1024),
-    )(lengths, route, around, w1, par, w2)
+    )(lengths, route, around, w1, *rows, w2)
     return jnp.transpose(out, (0, 2, 1, 3))[:, :, :, None, :]
 
 

time: 29.5 us -> 27.3 us (0.925)
  local copies, waits for them, and re-layouts: 4.75 us -> 3.32 us
  other arithmetic: 0.79 us -> 0 us
    another operation x1 -> x0, other arithmetic: 0.76 us -> none  [local(): par = jnp.stack([b_in, gain, b_mid], axis=1)]
    transpose x1 -> x0, local copies, waits for them, and re-layouts: 0.76 us -> none  [local(): taps = jnp.transpose(w_in, (0, 2, 4, 3, 1)).reshape(ch, 3, 3, 9)]
    unnamed x10 -> x16, local copies, waits for them, and re-layouts: 2.3 us -> 2.05 us
where the time goes in v2:
time: 27.3 us; the launch traced here: 27.1 us
  Pallas kernels  23.7 us (87%)
  local copies, waits for them, and re-layouts  3.32 us (12%)
    pallas_call x1, Pallas kernels, local(): pl.pallas_call(functools.partial(gather_kernel, groups, heights), out_sha...  15.6 us
    pallas_call x1, Pallas kernels, local(): pl.pallas_call(functools.partial(encode_kernel, groups, heights), out_sha...  8.05 us
    unnamed x16, local copies, waits for them, and re-layouts  2.05 us
    broadcast_in_dim x1, local copies, waits for them, and re-layouts, local(): return jnp.transpose(out, (0, 2, 1, 3))[:, :, :, None, :]  1.27 us

profile of v2, /device:TPU:0, one launch (start us, length us, event | category | flops | bytes accessed | tf_op | source)
XLA Modules:
  0.0 27.1 jit_solution(7293873636736552478)
XLA Ops:
  0.0 0.0 copy-start.2
  0.0 0.0 copy-start.3
  0.0 0.0 copy-start.4
  0.0 0.0 copy-start.5
  0.0 0.0 copy-start.6
  0.0 0.0 copy-start.7
  0.0 15.6 %shard_map.82.pix_ref = bf16[2,5,4,2,3,384]{5,4,3,2,1,0:T(4,128)(2,1)} custom-call(s32[16]{0:T(128)} %route_ref.3, bf16[4,3,2,384]{3,2,1,0:T(2,128)(2,1)} %bitcast.15), custom_call_target="tpu_custom_call" | custom-call | tf_op jit(solution)/shard_map/pallas_call | solution.py:183
  15.7 0.0 copy-done.2
  15.7 0.0 copy-done.3
  15.7 0.0 copy-done.4
  15.7 0.0 copy-done.5
  15.7 0.0 copy-done.6
  15.7 0.0 copy-done.7
  15.7 0.0 copy-start
  15.7 0.9 %copy-done = bf16[2,5,4,2,3,384]{5,4,3,2,1,0:T(4,128)(2,1)S(1)} copy-done((bf16[2,5,4,2,3,384]{5,4,3,2,1,0:T(4,128)(2,1)S(1)}, bf16[2,5,4,2,3,384]{5,4,3,2,1,0:T(4,128)(2,1)}, u32[]{:S(2)}) %copy-start) | copy-done | bytes 184344
  16.7 0.0 copy-start.1
  16.7 1.1 %copy-done.1 = bf16[96,96,3,3,3]{1,0,4,3,2:T(8,128)(2,1)S(1)} copy-done((bf16[96,96,3,3,3]{1,0,4,3,2:T(8,128)(2,1)S(1)}, bf16[96,96,3,3,3]{1,0,4,3,2:T(8,128)(2,1)}, u32[]{:S(2)}) %copy-start.1) | copy-done | bytes 497688
  17.8 8.0 %shard_map.83 = bf16[4,2,96,384]{3,2,1,0:T(8,128)(2,1)S(1)} custom-call(s32[16]{0:T(128)S(1)} %copy-done.4, s32[16]{0:T(128)S(1)} %copy-done.3, bf16[2,5,4,2,3,384]{5,4,3,2,1,0:T(4,128)(2,1)S(1)} %copy-done, bf16[3,3,3,3,96]{4,3,2,1,0:T(4,128)(2,1)S(1)} %bitcast.11, f32[1,96]{1,0:T(1,128)S(1)} %bitcast.12, f32[1,96]{1,0:T(1,128)S(1)} %bitcast.13, ...), custom_call_target="tpu_custom_call" | custom-call | tf_op jit(solution)/shard_map/pallas_call | solution.py:200
  25.8 1.3 %copy.9 = bf16[4,96,2,1,384]{4,2,3,1,0:T(2,128)(2,1)} copy(bf16[4,96,2,1,384]{4,1,2,0,3:T(8,128)(2,1)S(1)} %bitcast.9) | data formatting | bytes 1179648 | tf_op jit(solution)/shard_map/broadcast_in_dim | solution.py:216
Async XLA Ops:
  0.0 15.7 %copy-start.2 = (bf16[96,3,3,3,3]{0,4,3,2,1:T(4,128)(2,1)S(1)}, bf16[96,3,3,3,3]{0,4,3,2,1:T(4,128)(2,1)}, u32[]{:S(2)}) copy-start(bf16[96,3,3,3,3]{0,4,3,2,1:T(4,128)(2,1)} %param.11) | copy-start | bytes 46660
  0.0 15.7 %copy-start.3 = (s32[16]{0:T(128)S(1)}, s32[16]{0:T(128)}, u32[]{:S(2)}) copy-start(s32[16]{0:T(128)} %route_ref.3) | copy-start | bytes 196
  0.0 15.7 %copy-start.4 = (s32[16]{0:T(128)S(1)}, s32[16]{0:T(128)}, u32[]{:S(2)}) copy-start(s32[16]{0:T(128)} %lengths_ref.1) | copy-start | bytes 196
  0.0 15.7 %copy-start.5 = (f32[96]{0:T(128)S(1)}, f32[96]{0:T(128)}, u32[]{:S(2)}) copy-start(f32[96]{0:T(128)} %param.12) | copy-start | bytes 1156
  0.0 15.7 %copy-start.6 = (f32[96]{0:T(128)S(1)}, f32[96]{0:T(128)}, u32[]{:S(2)}) copy-start(f32[96]{0:T(128)} %param.13) | copy-start | bytes 1156
  0.0 15.7 %copy-start.7 = (f32[96]{0:T(128)S(1)}, f32[96]{0:T(128)}, u32[]{:S(2)}) copy-start(f32[96]{0:T(128)} %param.15) | copy-start | bytes 1156
  15.7 0.9 %copy-start = (bf16[2,5,4,2,3,384]{5,4,3,2,1,0:T(4,128)(2,1)S(1)}, bf16[2,5,4,2,3,384]{5,4,3,2,1,0:T(4,128)(2,1)}, u32[]{:S(2)}) copy-start(bf16[2,5,4,2,3,384]{5,4,3,2,1,0:T(4,128)(2,1)} %shard_map.82.pix_ref) | copy-start | bytes 552964
  16.7 1.1 %copy-start.1 = (bf16[96,96,3,3,3]{1,0,4,3,2:T(8,128)(2,1)S(1)}, bf16[96,96,3,3,3]{1,0,4,3,2:T(8,128)(2,1)}, u32[]{:S(2)}) copy-start(bf16[96,96,3,3,3]{1,0,4,3,2:T(8,128)(2,1)} %param.14) | copy-start | bytes 1492996

commit v3 on v2

--- a/solution.py
+++ b/solution.py
@@ -11,7 +11,7 @@
 REACH = (-2, -1, 1, 2)
 
 
-def gather_kernel(groups, heights, route_ref, pix_ref, out_ref, send, s1, r1, s2, r2):
+def gather(groups, heights, prepare, route_ref, pix_ref, out_ref, send, s1, r1, s2, r2):
     clip = lax.axis_index("clip")
     tm = lax.axis_index("tm")
     h = lax.axis_index("height")
@@ -83,6 +83,7 @@
         @pl.when(jnp.logical_and(there(dz), jnp.logical_or(j == 1, tm == 0)))
         def _(j=j, dz=dz):
             out_going(j, dz).start()
+    prepare()
     for copy in first:
         copy.wait_send()
     for j, dz in hops:
@@ -95,8 +96,12 @@
             out_going(j, dz).wait_send()
 
 
-def encode_kernel(groups, heights, lengths_ref, route_ref, pix_ref, taps_ref, b_in_ref, gain_ref, b_mid_ref, w2_ref, out_ref,
-                  grid, cols, acts, wide, tall, w1_ref, rows):
+def kernel(groups, heights, lengths_ref, route_ref, own_ref, taps_hbm, b_in_ref, gain_ref, b_mid_ref, w2_hbm, out_ref,
+           pix_ref, taps_ref, w2_ref, grid, cols, acts, wide, tall, w1_ref, rows, loaded, *sent):
+    load_taps = pltpu.make_async_copy(taps_hbm, taps_ref, loaded.at[0])
+    load_w2 = pltpu.make_async_copy(w2_hbm, w2_ref, loaded.at[1])
+    load_taps.start()
+    load_w2.start()
     ch = b_in_ref.shape[1]
     width = pix_ref.shape[-1]
     clip = lax.axis_index("clip")
@@ -115,23 +120,28 @@
     def left(v):
         return jnp.where(lane == width - 1, 0.0, pltpu.roll(v, width - 1, 1))
 
-    tall[...] = jnp.zeros_like(tall)
-    for i in range(3):
+    def prepare():
+        load_taps.wait()
+        tall[...] = jnp.zeros_like(tall)
+        for i in range(3):
+            for dt in range(3):
+                for dr in range(3):
+                    piece = taps_ref[i, dt, dr].astype(F32)
+                    for r in range(3):
+                        for dc in range(3):
+                            at = dt * 48 + dc * 16 + (r + dr) * 3 + i
+                            tall[at:at + 1, r * 128:r * 128 + ch] = piece[dc:dc + 1]
+        for r in range(3):
+            w1_ref[r * ch:(r + 1) * ch, :] = tall[:, r * 128:(r + 1) * 128].T[:ch].astype(BF16)
+        load_w2.wait()
+        wide[...] = jnp.zeros_like(wide)
         for dt in range(3):
             for dr in range(3):
-                piece = taps_ref[i, dt, dr].astype(F32)
-                for r in range(3):
-                    for dc in range(3):
-                        at = dt * 48 + dc * 16 + (r + dr) * 3 + i
-                        tall[at:at + 1, r * 128:r * 128 + ch] = piece[dc:dc + 1]
-    for r in range(3):
-        w1_ref[r * ch:(r + 1) * ch, :] = tall[:, r * 128:(r + 1) * 128].T[:ch].astype(BF16)
-    wide[...] = jnp.zeros_like(wide)
-    for dt in range(3):
-        for dr in range(3):
-            for dc in range(3):
-                at = (dt * 3 + dr) * 128
-                wide[dc * ch:(dc + 1) * ch, at:at + ch] = w2_ref[dt, dr, dc]
+                for dc in range(3):
+                    at = (dt * 3 + dr) * 128
+                    wide[dc * ch:(dc + 1) * ch, at:at + ch] = w2_ref[dt, dr, dc]
+
+    gather(groups, heights, prepare, route_ref, own_ref, pix_ref, *sent)
 
     def one(c, carry):
         grid[...] = jnp.zeros_like(grid)
@@ -178,31 +188,21 @@
     clips, colours, frames, _, width = pixels.shape
     ch = w_in.shape[0]
     vmem = pl.BlockSpec(memory_space=pltpu.VMEM)
+    hbm = pl.BlockSpec(memory_space=pltpu.HBM)
     smem = pl.BlockSpec(memory_space=pltpu.SMEM)
     pix = pixels.reshape(clips, colours, frames, width)
-    around = pl.pallas_call(
-        functools.partial(gather_kernel, groups, heights),
-        out_shape=jax.ShapeDtypeStruct((2, 5, clips, frames, colours, width), BF16),
-        in_specs=[smem, vmem],
-        out_specs=vmem,
-        scratch_shapes=[
-            pltpu.VMEM((groups, frames, colours, width), BF16),
-            pltpu.SemaphoreType.DMA((groups,)),
-            pltpu.SemaphoreType.DMA((groups,)),
-            pltpu.SemaphoreType.DMA((2, 5)),
-            pltpu.SemaphoreType.DMA((2, 5)),
-        ],
-        compiler_params=pltpu.CompilerParams(collective_id=0, has_side_effects=True),
-    )(route, pix)
     w1 = jnp.transpose(w_in, (1, 2, 3, 4, 0))
     rows = [v.reshape(1, ch) for v in (b_in, gain, b_mid)]
     w2 = jnp.transpose(w_mid, (2, 3, 4, 0, 1))
     out = pl.pallas_call(
-        functools.partial(encode_kernel, groups, heights),
+        functools.partial(kernel, groups, heights),
         out_shape=jax.ShapeDtypeStruct((clips, frames, ch, width), BF16),
-        in_specs=[smem, smem] + [vmem] * 6,
+        in_specs=[smem, smem, vmem, hbm, vmem, vmem, vmem, hbm],
         out_specs=vmem,
         scratch_shapes=[
+            pltpu.VMEM((2, 5, clips, frames, colours, width), BF16),
+            pltpu.VMEM(w1.shape, BF16),
+            pltpu.VMEM(w2.shape, BF16),
             pltpu.VMEM((6, 16, width), F32),
             pltpu.VMEM((288, width), BF16),
             pltpu.VMEM((12 * 128, width), BF16),
@@ -210,9 +210,15 @@
             pltpu.VMEM((144, 3 * 128), F32),
             pltpu.VMEM((3 * ch, 144), BF16),
             pltpu.VMEM((8, 128), F32),
+            pltpu.SemaphoreType.DMA((2,)),
+            pltpu.VMEM((groups, frames, colours, width), BF16),
+            pltpu.SemaphoreType.DMA((groups,)),
+            pltpu.SemaphoreType.DMA((groups,)),
+            pltpu.SemaphoreType.DMA((2, 5)),
+            pltpu.SemaphoreType.DMA((2, 5)),
         ],
-        compiler_params=pltpu.CompilerParams(vmem_limit_bytes=32 * 1024 * 1024),
-    )(lengths, route, around, w1, *rows, w2)
+        compiler_params=pltpu.CompilerParams(collective_id=0, has_side_effects=True, vmem_limit_bytes=60 * 1024 * 1024),
+    )(lengths, route, pix, w1, *rows, w2)
     return jnp.transpose(out, (0, 2, 1, 3))[:, :, :, None, :]
 
 

time: 27.3 us -> 25.6 us (0.938)
  local copies, waits for them, and re-layouts: 3.32 us -> 2.33 us
  Pallas kernels: 23.7 us -> 23.1 us
    unnamed x16 -> x0, local copies, waits for them, and re-layouts: 2.05 us -> none
    broadcast_in_dim x1, local copies, waits for them, and re-layouts: 1.27 us -> 2.33 us  [local(): return jnp.transpose(out, (0, 2, 1, 3))[:, :, :, None, :]]
    pallas_call x2 -> x1, Pallas kernels: 23.7 us -> 23.1 us  [local(): pl.pallas_call(functools.partial(kernel, groups, heights), out_shape=jax....]
where the time goes in v3:
time: 25.6 us; the launch traced here: 25.4 us
  Pallas kernels  23.1 us (90%)
  local copies, waits for them, and re-layouts  2.33 us (9%)
    pallas_call x1, Pallas kernels, local(): pl.pallas_call(functools.partial(kernel, groups, heights), out_shape=jax....  23.1 us
    broadcast_in_dim x1, local copies, waits for them, and re-layouts, local(): return jnp.transpose(out, (0, 2, 1, 3))[:, :, :, None, :]  2.33 us

profile of v3, /device:TPU:0, one launch (start us, length us, event | category | flops | bytes accessed | tf_op | source)
XLA Modules:
  0.0 25.4 jit_solution(12206643821386183182)
XLA Ops:
  0.0 23.1 %shard_map.82 = bf16[4,2,96,384]{3,2,1,0:T(8,128)(2,1)} custom-call(s32[16]{0:T(128)} %lengths_ref.1, s32[16]{0:T(128)} %route_ref.1, bf16[4,3,2,384]{3,2,1,0:T(2,128)(2,1)} %bitcast.12, bf16[3,3,3,3,96]{4,3,2,1,0:T(4,128)(2,1)} %bitcast.11, f32[1,96]{1,0:T(1,128)} %bitcast.13, f32[1,96]{1,0:T(1,128)} %bitcast.14, f32[1,96]{1,0:T(1,128)} %bitcast.15, ...), custom_call_target="tpu_custom_call" | custom-call | tf_op jit(solution)/shard_map/pallas_call | solution.py:197
  23.1 2.3 %copy.9 = bf16[4,96,2,1,384]{4,2,3,1,0:T(2,128)(2,1)} copy(bf16[4,96,2,1,384]{4,1,2,0,3:T(8,128)(2,1)} %bitcast.9) | data formatting | bytes 1179648 | tf_op jit(solution)/shard_map/broadcast_in_dim | solution.py:222

commit v4 on v3

--- a/solution.py
+++ b/solution.py
@@ -217,7 +217,7 @@
             pltpu.SemaphoreType.DMA((2, 5)),
             pltpu.SemaphoreType.DMA((2, 5)),
         ],
-        compiler_params=pltpu.CompilerParams(collective_id=0, has_side_effects=True, vmem_limit_bytes=60 * 1024 * 1024),
+        compiler_params=pltpu.CompilerParams(collective_id=0, has_side_effects=True, vmem_limit_bytes=54208 * 1024),
     )(lengths, route, pix, w1, *rows, w2)
     return jnp.transpose(out, (0, 2, 1, 3))[:, :, :, None, :]
 

time: 25.6 us -> 25.7 us (level)
  local copies, waits for them, and re-layouts: 2.33 us -> 3.45 us
  Pallas kernels: 23.1 us -> 22 us
    unnamed x0 -> x14, local copies, waits for them, and re-layouts: none -> 2.18 us
    pallas_call x1, Pallas kernels: 23.1 us -> 22 us  [local(): pl.pallas_call(functools.partial(kernel, groups, heights), out_shape=jax....]
    broadcast_in_dim x1, local copies, waits for them, and re-layouts: 2.33 us -> 1.27 us  [local(): return jnp.transpose(out, (0, 2, 1, 3))[:, :, :, None, :]]
where the time goes in v4:
time: 25.7 us; the launch traced here: 25.5 us
  Pallas kernels  22 us (86%)
  local copies, waits for them, and re-layouts  3.45 us (13%)
    pallas_call x1, Pallas kernels, local(): pl.pallas_call(functools.partial(kernel, groups, heights), out_shape=jax....  22 us
    unnamed x14, local copies, waits for them, and re-layouts  2.18 us
    broadcast_in_dim x1, local copies, waits for them, and re-layouts, local(): return jnp.transpose(out, (0, 2, 1, 3))[:, :, :, None, :]  1.27 us

profile of v4, /device:TPU:0, one launch (start us, length us, event | category | flops | bytes accessed | tf_op | source)
XLA Modules:
  0.0 25.5 jit_solution(6514141409011805133)
XLA Ops:
  0.0 0.0 copy-start.5
  0.0 0.0 copy-start.6
  0.0 0.0 copy-start.2
  0.0 0.0 copy-start.3
  0.0 0.0 copy-start.4
  0.0 0.6 %copy-done.5 = f32[96]{0:T(128)S(1)} copy-done((f32[96]{0:T(128)S(1)}, f32[96]{0:T(128)}, u32[]{:S(2)}) %copy-start.5) | copy-done | bytes 408
  0.7 0.0 copy-done.6
  0.7 0.0 copy-done.2
  0.7 0.0 copy-done.3
  0.7 0.0 copy-done.4
  0.7 0.0 copy-start
  0.7 0.7 %copy-done = bf16[96,3,3,3,3]{0,4,3,2,1:T(4,128)(2,1)S(1)} copy-done((bf16[96,3,3,3,3]{0,4,3,2,1:T(4,128)(2,1)S(1)}, bf16[96,3,3,3,3]{0,4,3,2,1:T(4,128)(2,1)}, u32[]{:S(2)}) %copy-start) | copy-done | bytes 15576
  1.5 0.0 copy-start.1
  1.5 0.7 %copy-done.1 = bf16[4,3,2,1,384]{4,2,3,1,0:T(2,128)(2,1)S(1)} copy-done((bf16[4,3,2,1,384]{4,2,3,1,0:T(2,128)(2,1)S(1)}, bf16[4,3,2,1,384]{4,2,3,1,0:T(2,128)(2,1)}, u32[]{:S(2)}) %copy-start.1) | copy-done | bytes 18456
  2.2 22.0 %shard_map.82 = bf16[4,2,96,384]{3,2,1,0:T(8,128)(2,1)S(1)} custom-call(s32[16]{0:T(128)S(1)} %copy-done.2, s32[16]{0:T(128)S(1)} %copy-done.3, bf16[4,3,2,384]{3,2,1,0:T(2,128)(2,1)S(1)} %bitcast.11, bf16[3,3,3,3,96]{4,3,2,1,0:T(4,128)(2,1)S(1)} %bitcast.10, f32[1,96]{1,0:T(1,128)S(1)} %bitcast.12, f32[1,96]{1,0:T(1,128)S(1)} %bitcast.13, ...), custom_call_target="tpu_custom_call" | custom-call | tf_op jit(solution)/shard_map/pallas_call | solution.py:197
  24.2 1.3 %copy.9 = bf16[4,96,2,1,384]{4,2,3,1,0:T(2,128)(2,1)} copy(bf16[4,96,2,1,384]{4,1,2,0,3:T(8,128)(2,1)S(1)} %bitcast.9) | data formatting | bytes 1179648 | tf_op jit(solution)/shard_map/broadcast_in_dim | solution.py:222
Async XLA Ops:
  0.0 0.7 %copy-start.5 = (f32[96]{0:T(128)S(1)}, f32[96]{0:T(128)}, u32[]{:S(2)}) copy-start(f32[96]{0:T(128)} %param.13) | copy-start | bytes 1156
  0.0 0.7 %copy-start.6 = (f32[96]{0:T(128)S(1)}, f32[96]{0:T(128)}, u32[]{:S(2)}) copy-start(f32[96]{0:T(128)} %param.15) | copy-start | bytes 1156
  0.0 0.7 %copy-start.2 = (s32[16]{0:T(128)S(1)}, s32[16]{0:T(128)}, u32[]{:S(2)}) copy-start(s32[16]{0:T(128)} %lengths_ref.1) | copy-start | bytes 196
  0.0 0.7 %copy-start.3 = (s32[16]{0:T(128)S(1)}, s32[16]{0:T(128)}, u32[]{:S(2)}) copy-start(s32[16]{0:T(128)} %route_ref.1) | copy-start | bytes 196
  0.0 0.7 %copy-start.4 = (f32[96]{0:T(128)S(1)}, f32[96]{0:T(128)}, u32[]{:S(2)}) copy-start(f32[96]{0:T(128)} %param.12) | copy-start | bytes 1156
  0.7 0.7 %copy-start = (bf16[96,3,3,3,3]{0,4,3,2,1:T(4,128)(2,1)S(1)}, bf16[96,3,3,3,3]{0,4,3,2,1:T(4,128)(2,1)}, u32[]{:S(2)}) copy-start(bf16[96,3,3,3,3]{0,4,3,2,1:T(4,128)(2,1)} %param.11) | copy-start | bytes 46660
  1.5 0.7 %copy-start.1 = (bf16[4,3,2,1,384]{4,2,3,1,0:T(2,128)(2,1)S(1)}, bf16[4,3,2,1,384]{4,2,3,1,0:T(2,128)(2,1)}, u32[]{:S(2)}) copy-start(bf16[4,3,2,1,384]{4,2,3,1,0:T(2,128)(2,1)} %param.8) | copy-start | bytes 55300

commit v5 on v4

--- a/solution.py
+++ b/solution.py
@@ -196,7 +196,7 @@
     w2 = jnp.transpose(w_mid, (2, 3, 4, 0, 1))
     out = pl.pallas_call(
         functools.partial(kernel, groups, heights),
-        out_shape=jax.ShapeDtypeStruct((clips, frames, ch, width), BF16),
+        out_shape=pltpu.VMEM((clips, frames, ch, width), BF16),
         in_specs=[smem, smem, vmem, hbm, vmem, vmem, vmem, hbm],
         out_specs=vmem,
         scratch_shapes=[
@@ -217,7 +217,7 @@
             pltpu.SemaphoreType.DMA((2, 5)),
             pltpu.SemaphoreType.DMA((2, 5)),
         ],
-        compiler_params=pltpu.CompilerParams(collective_id=0, has_side_effects=True, vmem_limit_bytes=54208 * 1024),
+        compiler_params=pltpu.CompilerParams(collective_id=0, has_side_effects=True, vmem_limit_bytes=56 * 1024 * 1024),
     )(lengths, route, pix, w1, *rows, w2)
     return jnp.transpose(out, (0, 2, 1, 3))[:, :, :, None, :]
 

time: 25.7 us -> 23.7 us (0.922)
  local copies, waits for them, and re-layouts: 3.45 us -> 1.27 us
  Pallas kernels: 22 us -> 22.3 us
    unnamed x14 -> x0, local copies, waits for them, and re-layouts: 2.18 us -> none
    pallas_call x1, Pallas kernels: 22 us -> 22.3 us  [local(): pl.pallas_call(functools.partial(kernel, groups, heights), out_shape=pltp...]
where the time goes in v5:
time: 23.7 us; the launch traced here: 23.5 us
  Pallas kernels  22.3 us (94%)
  local copies, waits for them, and re-layouts  1.27 us (5%)
    pallas_call x1, Pallas kernels, local(): pl.pallas_call(functools.partial(kernel, groups, heights), out_shape=pltp...  22.3 us
    broadcast_in_dim x1, local copies, waits for them, and re-layouts, local(): return jnp.transpose(out, (0, 2, 1, 3))[:, :, :, None, :]  1.27 us

profile of v5, /device:TPU:0, one launch (start us, length us, event | category | flops | bytes accessed | tf_op | source)
XLA Modules:
  0.0 23.5 jit_solution(16353828059473886569)
XLA Ops:
  0.0 22.3 %shard_map.82 = bf16[4,2,96,384]{3,2,1,0:T(8,128)(2,1)S(1)} custom-call(s32[16]{0:T(128)} %lengths_ref.1, s32[16]{0:T(128)} %route_ref.1, bf16[4,3,2,384]{3,2,1,0:T(2,128)(2,1)} %bitcast.12, bf16[3,3,3,3,96]{4,3,2,1,0:T(4,128)(2,1)} %bitcast.11, f32[1,96]{1,0:T(1,128)} %bitcast.13, f32[1,96]{1,0:T(1,128)} %bitcast.14, f32[1,96]{1,0:T(1,128)} %bitcast.15, ...), custom_call_target="tpu_custom_call" | custom-call | tf_op jit(solution)/shard_map/pallas_call | solution.py:197
  22.3 1.3 %copy.9 = bf16[4,96,2,1,384]{4,2,3,1,0:T(2,128)(2,1)} copy(bf16[4,96,2,1,384]{4,1,2,0,3:T(8,128)(2,1)S(1)} %bitcast.9) | data formatting | bytes 1179648 | tf_op jit(solution)/shard_map/broadcast_in_dim | solution.py:222
